TPU v7x, 32 devices: a whole 2x2x4 slice. The times are simulated.
32 devices in a mesh: groups: 2 (over y), ctx: 4 (over z), head: 4 (over x, core).
Axes of the slice: x: 2, y: 2, z: 4, core: 2. Of those that a mesh axis runs over, the one named last changes fastest.
Arguments:
- queries: bfloat16 [64, 2048, 128], P(('groups', 'head'), 'ctx'), parts along dimension 0, may hold values from -48 to 48
- key_rows: bfloat16 [8, 2048, 128], P(('groups', 'head'), 'ctx'), parts along dimension 0, may hold values from -6 to 6
- value_rows: bfloat16 [8, 2048, 128], P(('groups', 'head'), 'ctx'), parts along dimension 0, may hold values from -6 to 6
- out_grad: bfloat16 [64, 2048, 128], P(('groups', 'head'), 'ctx'), parts along dimension 0, may hold values from -6 to 6
- link_mask: int32 [32, 11], P(('groups', 'ctx')), parts along dimension 0, may hold values from 0 to 1, as said below
Outputs:
- output: bfloat16 [64, 2048, 128], P(('groups', 'head'), 'ctx'), parts along dimension 0
- query_grad: bfloat16 [64, 2048, 128], P(('groups', 'head'), 'ctx'), parts along dimension 0
- key_grad: bfloat16 [8, 2048, 128], P(('groups', 'head'), 'ctx'), parts along dimension 0
- value_grad: bfloat16 [8, 2048, 128], P(('groups', 'head'), 'ctx'), parts along dimension 0
There are 2 independent parts, one for each index of `groups`. A program takes and returns all parts, laid end to end along the dimension named above; each array names one. Nothing has to cross between parts.
Inputs may be any that keep to these rules, and one draw needn't show every extreme that they name: `link_mask`: column 0 is 1 in every row.
All inputs are finite; a program needn't handle non-finite values.
Results may differ from a plain program's by a relative error of at most 0.028.
Values may be sent and summed in bfloat16 or wider, within the bound.
A program may use at most 64 MiB of HBM per device.

v0:
```python
import math

import jax
import jax.numpy as jnp
from jax import lax
from jax.sharding import PartitionSpec as P

BLK = 128
NOFF = 11


def from_behind(value, axis, steps):
    count = lax.axis_size(axis)
    first, last = (max(0, -steps), min(count, count - steps))
    return lax.ppermute(value, axis, [(source, source + steps) for source in range(first, last)])


def slot_table(block_count, ctx_size):
    entries = []
    for slot_id in range(NOFF):
        offset = 0 if slot_id == 0 else 2 ** (slot_id - 1)
        if offset < block_count:
            entries.append((slot_id, offset, 0))
        elif offset // block_count < ctx_size:
            entries.append((slot_id, offset, offset // block_count))
    return entries


def near_piece(local_blocks, prev_blocks, offset, first_block, span_count):
    block_count = local_blocks.shape[0]
    last_block = first_block + span_count
    middle = min(max(offset, first_block), last_block)
    pieces = []
    if middle > first_block:
        pieces.append(
            prev_blocks[first_block - offset + block_count : middle - offset + block_count]
        )
    if last_block > middle:
        pieces.append(local_blocks[middle - offset : last_block - offset])
    if len(pieces) > 1:
        return jnp.concatenate(pieces, axis=0)
    return pieces[0]


def local(queries, key_rows, value_rows, out_grad, link_mask):
    heads_local, row_count, head_size = queries.shape
    block_count = row_count // BLK
    ctx_size = lax.axis_size("ctx")
    device_index = lax.axis_index("ctx")
    inv_root = 1.0 / math.sqrt(head_size)
    key_value = jnp.concatenate([key_rows[0], value_rows[0]], axis=1)
    entries = slot_table(block_count, ctx_size)
    distances = sorted(set((entry[2] for entry in entries if entry[2] > 0)))
    copies = {}
    for distance in distances:
        copies[distance] = from_behind(key_value, "ctx", distance)

    def to_blocks(array):
        return array.reshape(block_count, BLK, 2 * head_size)

    local_blocks = to_blocks(key_value)
    far_blocks = {distance: to_blocks(copies[distance]) for distance in distances}
    prev_blocks = far_blocks[1]
    own_grads = jnp.zeros((block_count, BLK, 2 * head_size), jnp.float32)
    pending = {
        distance: jnp.zeros((block_count, BLK, 2 * head_size), jnp.float32)
        for distance in distances
    }
    causal = jnp.arange(BLK)[None, :] <= jnp.arange(BLK)[:, None]
    group_size = min(block_count, max(1, 512 // (heads_local * BLK)))
    outputs = []
    query_grads = []
    for first_block in range(0, block_count, group_size):
        span_count = min(group_size, block_count - first_block)
        last_block = first_block + span_count
        block_ids = device_index * block_count + jnp.arange(first_block, last_block)
        pieces = []
        allowed = []
        for slot_id, offset, distance in entries:
            if distance == 0:
                pieces.append(
                    near_piece(local_blocks, prev_blocks, offset, first_block, span_count)
                )
            else:
                pieces.append(far_blocks[distance][first_block:last_block])
            link_live = (link_mask[first_block:last_block, slot_id] == 1) & (block_ids >= offset)
            if offset == 0:
                allowed.append(link_live[:, None, None] & causal[None])
            else:
                allowed.append(jnp.broadcast_to(link_live[:, None, None], (span_count, BLK, BLK)))
        gathered = jnp.concatenate(pieces, axis=1)
        key_part = gathered[..., :head_size]
        value_part = gathered[..., head_size:]
        mask_all = jnp.concatenate(allowed, axis=2)
        query_part = queries[:, first_block * BLK : last_block * BLK].reshape(
            heads_local, span_count, BLK, head_size
        )
        grad_part = out_grad[:, first_block * BLK : last_block * BLK].reshape(
            heads_local, span_count, BLK, head_size
        )
        scores = (
            jnp.einsum("hgtd,gkd->hgtk", query_part, key_part, preferred_element_type=jnp.float32)
            * inv_root
        )
        scores = jnp.where(mask_all[None], scores, -jnp.inf)
        row_max = jnp.max(scores, axis=-1, keepdims=True)
        log_total = row_max + jnp.log(jnp.sum(jnp.exp(scores - row_max), axis=-1, keepdims=True))
        weights = jnp.exp(scores - log_total)
        weights_low = weights.astype(jnp.bfloat16)
        output = jnp.einsum(
            "hgtk,gkd->hgtd", weights_low, value_part, preferred_element_type=jnp.float32
        ).astype(jnp.bfloat16)
        row_dot = jnp.sum(
            grad_part.astype(jnp.float32) * output.astype(jnp.float32), axis=-1, keepdims=True
        )
        grad_weights = jnp.einsum(
            "hgtd,gkd->hgtk", grad_part, value_part, preferred_element_type=jnp.float32
        )
        grad_scores = (weights * (grad_weights - row_dot) * inv_root).astype(jnp.bfloat16)
        query_grad = jnp.einsum(
            "hgtk,gkd->hgtd", grad_scores, key_part, preferred_element_type=jnp.float32
        ).astype(jnp.bfloat16)
        key_part_grad = jnp.einsum(
            "hgtk,hgtd->gkd", grad_scores, query_part, preferred_element_type=jnp.float32
        )
        value_part_grad = jnp.einsum(
            "hgtk,hgtd->gkd", weights_low, grad_part, preferred_element_type=jnp.float32
        )
        joined_grads = jnp.concatenate([key_part_grad, value_part_grad], axis=-1)
        joined_grads = joined_grads.reshape(span_count, len(entries), BLK, 2 * head_size)
        for position, (slot_id, offset, distance) in enumerate(entries):
            slot_grad = joined_grads[:, position]
            if distance > 0:
                pending[distance] = pending[distance].at[first_block:last_block].add(slot_grad)
            else:
                middle = min(max(offset, first_block), last_block)
                if middle > first_block:
                    pending[1] = (
                        pending[1]
                        .at[first_block - offset + block_count : middle - offset + block_count]
                        .add(slot_grad[: middle - first_block])
                    )
                if last_block > middle:
                    own_grads = own_grads.at[middle - offset : last_block - offset].add(
                        slot_grad[middle - first_block :]
                    )
        outputs.append(output.reshape(heads_local, span_count * BLK, head_size))
        query_grads.append(query_grad.reshape(heads_local, span_count * BLK, head_size))
    arrived = None
    for distance in reversed(distances):
        running = pending[distance] if arrived is None else pending[distance] + arrived
        arrived = from_behind(running, "ctx", -max(distance // 2, 1))
    own_grads = own_grads + arrived
    summed = own_grads.reshape(row_count, 2 * head_size)
    key_grad = summed[:, :head_size].astype(jnp.bfloat16)[None]
    value_grad = summed[:, head_size:].astype(jnp.bfloat16)[None]
    return (
        jnp.concatenate(outputs, axis=1),
        jnp.concatenate(query_grads, axis=1),
        key_grad,
        value_grad,
    )


def solution(mesh):
    return jax.shard_map(
        local,
        mesh=mesh,
        in_specs=(
            P(("groups", "head"), "ctx", None),
            P(("groups", "head"), "ctx", None),
            P(("groups", "head"), "ctx", None),
            P(("groups", "head"), "ctx", None),
            P(("groups", "ctx"), None),
        ),
        out_specs=(
            P(("groups", "head"), "ctx", None),
            P(("groups", "head"), "ctx", None),
            P(("groups", "head"), "ctx", None),
            P(("groups", "head"), "ctx", None),
        ),
        check_vma=False,
    )
```

profile of v0, /device:TPU:0, one launch (start us, length us, event | category | flops | bytes accessed | tf_op | source)
XLA Modules:
  0.0 84.7 jit_solution(2241499861576197564)
XLA Ops:
  0.6 1.7 %pad_maximum_fusion.2 = bf16[512,256]{1,0:T(8,128)(2,1)} fusion(bf16[512,128]{1,0:T(8,128)(2,1)} %bitcast.589, bf16[512,128]{1,0:T(8,128)(2,1)} %bitcast.593), kind=kLoop, calls=%fused_computation.115 | loop fusion | flops 524288 | bytes 524288 | tf_op jit(solution)/shard_map/concatenate | solution.py:51
  2.3 5.7 %collective-permute-start = (bf16[512,256]{1,0:T(8,128)(2,1)}, bf16[512,256]{1,0:T(8,128)(2,1)}, u32[]{:S(2)}, u32[]{:S(2)}) collective-permute-start(bf16[512,256]{1,0:T(8,128)(2,1)} %pad_maximum_fusion.2), channel_id=1, source_target_pairs={{0,4},{4,8},{8,12},{1,5},{5,9},{9,13},{2,6},{6,10},{10,14},{3,7},{... | collective-permute-start | bytes 786440 | tf_op jit(solution)/shard_map/ppermute | solution.py:15
  8.1 4.5 %collective-permute-start.1 = (bf16[512,256]{1,0:T(8,128)(2,1)}, bf16[512,256]{1,0:T(8,128)(2,1)}, u32[]{:S(2)}, u32[]{:S(2)}) collective-permute-start(bf16[512,256]{1,0:T(8,128)(2,1)} %pad_maximum_fusion.2), channel_id=1, source_target_pairs={{0,8},{4,12},{1,9},{5,13},{2,10},{6,14},{3,11},{7,15},{16,24},{20,... | collective-permute-start | bytes 786440 | tf_op jit(solution)/shard_map/ppermute | solution.py:15
  12.6 1.3 %slice.773 = s32[1,1]{1,0:T(1,128)} slice(s32[4,11]{1,0:T(4,128)} %param.49), slice={[3:4], [3:4]} | slice | bytes 8 | tf_op jit(solution)/shard_map/slice | solution.py:86
  13.9 2.1 %fusion.172 = (s32[1,1]{1,0:T(1,128)}, s32[1,1]{1,0:T(1,128)}, s32[1,1]{1,0:T(1,128)}, s32[1,1]{1,0:T(1,128)}, s32[1,1]{1,0:T(1,128)}, /*index=5*/s32[1,1]{1,0:T...) fusion(s32[4,11]{1,0:T(4,128)} %param.49), kind=kLoop, calls=%fused_computation.291 | loop fusion | bytes 152 | tf_op jit(solution)/shard_map/slice | solution.py:86
  16.0 0.8 constant_dynamic-update-slice_fusion.24
  29.6 1.3 %fusion.171 = (bf16[8,128,128]{2,1,0:T(8,128)(2,1)S(1)}, bf16[8,128,128]{2,1,0:T(8,128)(2,1)S(1)}, bf16[8,128,128]{2,1,0:T(8,128)(2,1)S(1)}, bf16[8,128,128]{2,1,0:T(8,128)(2,1)S(1)}) fusion(bf16[8,512,128]{2,1,0:T(8,128)(2,1)} %param.48), kind=kLoop, calls=%fused_computation.290 | loop fusion | bytes 2097152
  32.6 0.8 constant_dynamic-update-slice_fusion.3
  33.4 0.8 constant_dynamic-update-slice_fusion.2
  34.3 0.9 %constant_dynamic-update-slice_fusion.1 = (bf16[1,640,256]{2,1,0:T(8,128)(2,1)S(1)}, bf16[1,640,256]{2,1,0:T(8,128)(2,1)S(1)}, bf16[1,640,256]{2,1,0:T(8,128)(2,1)S(1)}, bf16[1,640,256]{2,1,0:T(8,128)(2,1)S(1)}) fusion(bf16[1,640,256]{2,1,0:T(8,128)(2,1)S(1)} %constant_dynamic-update-slice_fusion.2, bf16[512,256]{1,0:T(8,128)(2,1)} %collective-permute-done, ...), kind=kLoop, calls=%fused_computation.218 | loop fusion | bytes 458752
  35.2 0.8 constant_dynamic-update-slice_fusion.11
  36.1 1.0 %constant_dynamic-update-slice_fusion = (bf16[1,640,256]{2,1,0:T(8,128)(2,1)S(1)}, bf16[1,640,256]{2,1,0:T(8,128)(2,1)S(1)}, bf16[1,640,256]{2,1,0:T(8,128)(2,1)S(1)}, bf16[1,640,256]{2,1,0:T(8,128)(2,1)S(1)}) fusion(bf16[1,640,256]{2,1,0:T(8,128)(2,1)S(1)} %get-tuple-element.276, bf16[512,256]{1,0:T(8,128)(2,1)} %collective-permute-done.1, ...), kind=kLoop, calls=%fused_computation.217 | loop fusion | bytes 524288 | tf_op jit(solution)/shard_map/concatenate | solution.py:91
  39.2 0.8 fusion.7
  44.3 0.8 fusion.1
  48.5 0.8 fusion.3
  50.4 0.7 fusion.175
  52.3 0.7 fusion.5
  54.6 1.3 %collective-permute-start.2 = (f32[4,128,256]{1,2,0:T(8,128)S(1)}, f32[4,128,256]{1,2,0:T(8,128)S(1)}, u32[]{:S(2)}, u32[]{:S(2)}) collective-permute-start(f32[4,128,256]{1,2,0:T(8,128)S(1)} %get-tuple-element.256), channel_id=1, source_target_pairs={{4,0},{8,4},{12,8},{5,1},{9,5},{13,9},{6,2},{10,6},{14,10},{7,3},{... | collective-permute-start | bytes 1572872 | tf_op jit(solution)/shard_map/ppermute | solution.py:15
  57.2 1.0 %pad_maximum_fusion.1 = bf16[8,512,128]{2,1,0:T(8,128)(2,1)} fusion(bf16[8,128,128]{2,1,0:T(8,128)(2,1)S(1)} %fusion.52, bf16[8,128,128]{2,1,0:T(8,128)(2,1)S(1)} %fusion.55, bf16[8,128,128]{2,1,0:T(8,128)(2,1)S(1)} %fusion.58, bf16[8,128,128]{2,1,0:T(8,128)(2,1)S(1)} %fusion.61), kind=kLoop, calls=%fused_computation.69 | loop fusion | flops 4194304 | bytes 2097152 | tf_op jit(solution)/shard_map/concatenate | solution.py:159
  58.2 11.4 %collective-permute-done.2 = f32[4,128,256]{1,2,0:T(8,128)S(1)} collective-permute-done((f32[4,128,256]{1,2,0:T(8,128)S(1)}, f32[4,128,256]{1,2,0:T(8,128)S(1)}, u32[]{:S(2)}, u32[]{:S(2)}) %collective-permute-start.2) | collective-permute-done | bytes 524320 | tf_op jit(solution)/shard_map/ppermute | solution.py:15
  69.7 1.3 %collective-permute-start.3 = (f32[4,128,256]{1,2,0:T(8,128)S(1)}, f32[4,128,256]{1,2,0:T(8,128)S(1)}, u32[]{:S(2)}, u32[]{:S(2)}) collective-permute-start(f32[4,128,256]{1,2,0:T(8,128)S(1)} %add.227), channel_id=1, source_target_pairs={{4,0},{8,4},{12,8},{5,1},{9,5},{13,9},{6,2},{10,6},{14,10},{7,3},{... | collective-permute-start | bytes 1572872 | tf_op jit(solution)/shard_map/ppermute | solution.py:15
  71.2 1.3 %copy.75 = bf16[8,512,128]{2,1,0:T(8,128)(2,1)} copy(bf16[8,512,128]{1,2,0:T(8,128)(2,1)S(1)} %pad_maximum_fusion) | data formatting | bytes 2097152
  72.5 11.3 %collective-permute-done.3 = f32[4,128,256]{1,2,0:T(8,128)S(1)} collective-permute-done((f32[4,128,256]{1,2,0:T(8,128)S(1)}, f32[4,128,256]{1,2,0:T(8,128)S(1)}, u32[]{:S(2)}, u32[]{:S(2)}) %collective-permute-start.3) | collective-permute-done | bytes 524320 | tf_op jit(solution)/shard_map/ppermute | solution.py:15
  84.0 0.7 slice_bitcast_fusion.24
  (93 shorter events, 16.8 us)
Async XLA Ops:
  2.3 30.2 %copy-start.2 = (bf16[1,512,128]{2,1,0:T(8,128)(2,1)S(1)}, bf16[1,512,128]{2,1,0:T(8,128)(2,1)}, u32[]{:S(2)}) copy-start(bf16[1,512,128]{2,1,0:T(8,128)(2,1)} %param.47) | copy-start | bytes 393220
  2.3 30.2 %copy-start.3 = (bf16[1,512,128]{2,1,0:T(8,128)(2,1)S(1)}, bf16[1,512,128]{2,1,0:T(8,128)(2,1)}, u32[]{:S(2)}) copy-start(bf16[1,512,128]{2,1,0:T(8,128)(2,1)} %param.46) | copy-start | bytes 393220
  2.3 30.2 %collective-permute-start = (bf16[512,256]{1,0:T(8,128)(2,1)}, bf16[512,256]{1,0:T(8,128)(2,1)}, u32[]{:S(2)}, u32[]{:S(2)}) collective-permute-start(bf16[512,256]{1,0:T(8,128)(2,1)} %pad_maximum_fusion.2), channel_id=1, source_target_pairs={{0,4},{4,8},{8,12},{1,5},{5,9},{9,13},{2,6},{6,10},{10,14},{3,7},{... | collective-permute-start | bytes 786440 | tf_op jit(solution)/shard_map/ppermute | solution.py:15
  8.1 28.0 %collective-permute-start.1 = (bf16[512,256]{1,0:T(8,128)(2,1)}, bf16[512,256]{1,0:T(8,128)(2,1)}, u32[]{:S(2)}, u32[]{:S(2)}) collective-permute-start(bf16[512,256]{1,0:T(8,128)(2,1)} %pad_maximum_fusion.2), channel_id=1, source_target_pairs={{0,8},{4,12},{1,9},{5,13},{2,10},{6,14},{3,11},{7,15},{16,24},{20,... | collective-permute-start | bytes 786440 | tf_op jit(solution)/shard_map/ppermute | solution.py:15
  30.8 6.2 %copy-start.1 = (bf16[8,512,128]{2,1,0:T(8,128)(2,1)S(1)}, bf16[8,512,128]{2,1,0:T(8,128)(2,1)}, u32[]{:S(2)}) copy-start(bf16[8,512,128]{2,1,0:T(8,128)(2,1)} %param.45) | copy-start | bytes 3145732
  31.0 0.6 copy-start.6
  31.1 0.6 copy-start.4
  37.9 1.2 %copy-start = (bf16[8,512,128]{2,1,0:T(8,128)(2,1)S(1)}, bf16[8,512,128]{2,1,0:T(8,128)(2,1)}, u32[]{:S(2)}) copy-start(bf16[8,512,128]{2,1,0:T(8,128)(2,1)} %param.48) | copy-start | bytes 3145732
  41.7 0.9 %copy-start.7 = (pred[1,128,640]{1,2,0:T(8,128)(4,1)S(1)}, pred[1,128,640]{1,2,0:T(8,128)(4,1)}, u32[]{:S(2)}) copy-start(pred[1,128,640]{1,2,0:T(8,128)(4,1)} %copy-done.6) | copy-start | bytes 245764
  45.0 1.8 %copy-start.5 = (pred[1,128,640]{1,2,0:T(8,128)(4,1)S(1)}, pred[1,128,640]{1,2,0:T(8,128)(4,1)}, u32[]{:S(2)}) copy-start(pred[1,128,640]{1,2,0:T(8,128)(4,1)} %copy-done.4) | copy-start | bytes 245764
  54.6 15.0 %collective-permute-start.2 = (f32[4,128,256]{1,2,0:T(8,128)S(1)}, f32[4,128,256]{1,2,0:T(8,128)S(1)}, u32[]{:S(2)}, u32[]{:S(2)}) collective-permute-start(f32[4,128,256]{1,2,0:T(8,128)S(1)} %get-tuple-element.256), channel_id=1, source_target_pairs={{4,0},{8,4},{12,8},{5,1},{9,5},{13,9},{6,2},{10,6},{14,10},{7,3},{... | collective-permute-start | bytes 1572872 | tf_op jit(solution)/shard_map/ppermute | solution.py:15
  69.7 14.1 %collective-permute-start.3 = (f32[4,128,256]{1,2,0:T(8,128)S(1)}, f32[4,128,256]{1,2,0:T(8,128)S(1)}, u32[]{:S(2)}, u32[]{:S(2)}) collective-permute-start(f32[4,128,256]{1,2,0:T(8,128)S(1)} %add.227), channel_id=1, source_target_pairs={{4,0},{8,4},{12,8},{5,1},{9,5},{13,9},{6,2},{10,6},{14,10},{7,3},{... | collective-permute-start | bytes 1572872 | tf_op jit(solution)/shard_map/ppermute | solution.py:15
where the time goes:
time: 85.6 us; the launch traced here: 84.7 us
  waiting for transfers between devices  22.7 us (27%)
  matrix products  14 us (16%)
  between operations  14 us (16%)
  local copies, waits for them, and re-layouts  13.9 us (16%)
  starting transfers between devices  12.8 us (15%)
  other arithmetic  7.31 us (9%)
    ppermute x4, waiting for transfers between devices, from_behind(): lax.ppermute(value, axis, [(source, source + steps) for source in range(f...  22.7 us
    ppermute x4, starting transfers between devices, from_behind(): lax.ppermute(value, axis, [(source, source + steps) for source in range(f...  12.8 us
    unnamed x38, local copies, waits for them, and re-layouts  8.52 us
    slice x2, local copies, waits for them, and re-layouts, local(): link_mask[first_block:last_block, slot_id] == 1  3.35 us
    dot_general x4, matrix products, local(): jnp.einsum('hgtd,gkd->hgtk', grad_part, value_part, preferred_element_typ...  3.01 us
    dot_general x4, matrix products, local(): jnp.einsum('hgtk,gkd->hgtd', grad_scores, key_part, preferred_element_typ...  2.47 us
    dot_general x4, matrix products, local(): jnp.einsum('hgtk,hgtd->gkd', grad_scores, query_part, preferred_element_t...  2.3 us
    dot_general x4, matrix products, local(): jnp.einsum('hgtk,hgtd->gkd', weights_low, grad_part, preferred_element_ty...  2.27 us
  transfers between devices with their start and end apart: 4, of which 2 were waited for; matrix products, arithmetic and copies ran while one was open for 16% of the time, Pallas kernels for 0%

commit v1 on v0

v1 whole, which is shorter than its diff:
```python
import functools
import math

import jax
import jax.numpy as jnp
from jax import lax
from jax.experimental import pallas as pl
from jax.experimental.pallas import tpu as pltpu
from jax.sharding import PartitionSpec as P

BLK = 128
NOFF = 11
MESH = pl.DeviceIdType.MESH
NEG = -1e30
F32 = jnp.float32
BF16 = jnp.bfloat16


def slot_table(block_count, ctx_size):
    entries = []
    for slot_id in range(NOFF):
        offset = 0 if slot_id == 0 else 2 ** (slot_id - 1)
        if offset < block_count:
            entries.append((slot_id, offset, 0))
        elif offset // block_count < ctx_size:
            entries.append((slot_id, offset, offset // block_count))
    return entries


def hop_of(distance):
    return max(distance // 2, 1)


def dot(a, b, dims):
    return lax.dot_general(a, b, (dims, ((), ())), preferred_element_type=F32)


def kernel(
    ctx_size,
    entries,
    distances,
    mask_ref,
    q_ref,
    g_ref,
    k_ref,
    v_ref,
    out_ref,
    dq_ref,
    dk_ref,
    dv_ref,
    own_kv,
    far_kv,
    own_grad,
    pend_grad,
    stage,
    landed,
    w_scr,
    ds_scr,
    kv_send,
    kv_recv,
    g_send,
    g_recv,
):
    me = lax.axis_index("ctx")
    heads, row_count, head_size = q_ref.shape
    block_count = row_count // BLK
    inv_root = 1.0 / math.sqrt(head_size)
    scale = inv_root * math.log2(math.e)
    place = {distance: i for i, distance in enumerate(distances)}

    def rows(block):
        return pl.ds(block * BLK, BLK)

    def kv_copy(distance, block):
        i = place[distance]
        if distance == 1:
            source = own_kv.at[rows(block)]
        else:
            source = far_kv.at[place[distance // 2], rows(block)]
        return pltpu.make_async_remote_copy(
            src_ref=source,
            dst_ref=far_kv.at[i, rows(block)],
            send_sem=kv_send.at[i, block],
            recv_sem=kv_recv.at[i, block],
            device_id={"ctx": me + hop_of(distance)},
            device_id_type=MESH,
        )

    def kv_sends(distance):
        hop = hop_of(distance)
        return (me + hop < ctx_size) & (me >= distance - hop) if distance > 1 else me + hop < ctx_size

    def grad_copy(distance, block):
        i = place[distance]
        return pltpu.make_async_remote_copy(
            src_ref=stage.at[i, rows(block)],
            dst_ref=landed.at[i, rows(block)],
            send_sem=g_send.at[i, block],
            recv_sem=g_recv.at[i, block],
            device_id={"ctx": me - hop_of(distance)},
            device_id_type=MESH,
        )

    def grad_arrives(distance):
        hop = hop_of(distance)
        return (me + hop < ctx_size) & (me + hop >= distance)

    own_kv[:, :head_size] = k_ref[0]
    own_kv[:, head_size:] = v_ref[0]
    for distance in distances:

        @pl.when(me < distance)
        def _(distance=distance):
            far_kv[place[distance]] = jnp.zeros(far_kv.shape[1:], BF16)

    hops = sorted(set(hop_of(distance) for distance in distances))
    barrier = pltpu.get_barrier_semaphore()
    for hop in hops:

        @pl.when(me + hop < ctx_size)
        def _(hop=hop):
            pl.semaphore_signal(barrier, inc=1, device_id={"ctx": me + hop}, device_id_type=MESH)

        @pl.when(me >= hop)
        def _(hop=hop):
            pl.semaphore_signal(barrier, inc=1, device_id={"ctx": me - hop}, device_id_type=MESH)

    peers = 0
    for hop in hops:
        peers = peers + (me + hop < ctx_size).astype(jnp.int32) + (me >= hop).astype(jnp.int32)
    pl.semaphore_wait(barrier, peers)

    first_order = [0] + list(range(block_count - 1, 0, -1))

    @pl.when(kv_sends(1))
    def _():
        for block in first_order:
            kv_copy(1, block).start()

    def receive(distance):
        for block in range(block_count):

            @pl.when(me >= distance)
            def _(block=block):
                kv_copy(distance, block).wait_recv()

            if 2 * distance in place:

                @pl.when(kv_sends(2 * distance))
                def _(block=block):
                    kv_copy(2 * distance, block).start()

    for distance in distances[:-1]:
        receive(distance)

    own_set = set()
    pend_set = set()

    def add_own(block, value_k, value_v):
        for part, value in ((slice(0, head_size), value_k), (slice(head_size, None), value_v)):
            if block in own_set:
                own_grad[rows(block), part] += value
            else:
                own_grad[rows(block), part] = value
        own_set.add(block)

    def add_pend(distance, block, value_k, value_v):
        i = place[distance]
        for part, value in ((slice(0, head_size), value_k), (slice(head_size, None), value_v)):
            if (i, block) in pend_set:
                pend_grad[i, rows(block), part] += value
            else:
                pend_grad[i, rows(block), part] = value
        pend_set.add((i, block))

    head_step = 2 if heads % 2 == 0 else 1
    step_rows = head_step * BLK

    def piece(block, offset, distance, part):
        if distance > 0:
            return far_kv[place[distance], rows(block), part]
        if block >= offset:
            return own_kv[rows(block - offset), part]
        return far_kv[place[1], rows(block - offset + block_count), part]

    def compute(block):
        keys = jnp.concatenate(
            [piece(block, offset, distance, slice(0, head_size)) for _, offset, distance in entries],
            axis=0,
        )
        values = jnp.concatenate(
            [
                piece(block, offset, distance, slice(head_size, None))
                for _, offset, distance in entries
            ],
            axis=0,
        )
        block_id = me * block_count + block
        row_ids = lax.broadcasted_iota(jnp.int32, (step_rows, BLK), 0) % BLK
        causal = lax.broadcasted_iota(jnp.int32, (step_rows, BLK), 1) <= row_ids
        bias = []
        for slot_id, offset, _ in entries:
            live = (mask_ref[block, slot_id] == 1) & (block_id >= offset)
            bias.append(jnp.where(live, 0.0, NEG).astype(F32))
        for step in range(heads // head_step):
            part = (slice(step * head_step, (step + 1) * head_step), rows(block))
            q = q_ref[part].reshape(step_rows, head_size)
            g = g_ref[part].reshape(step_rows, head_size)
            s = dot(q, keys, ((1,), (1,)))
            pieces = []
            top = None
            for position, (slot_id, offset, _) in enumerate(entries):
                t = s[:, position * BLK : (position + 1) * BLK]
                if offset == 0:
                    t = jnp.where(causal, t, NEG)
                else:
                    t = t + bias[position]
                pieces.append(t)
                top = t if top is None else jnp.maximum(top, t)
            top = jnp.max(top, axis=1, keepdims=True) * scale
            p = jnp.exp2(jnp.concatenate(pieces, axis=1) * scale - top)
            total = jnp.sum(p, axis=1, keepdims=True)
            w = p * (1.0 / total)
            w_low = w.astype(BF16)
            out = dot(w_low, values, ((1,), (0,))).astype(BF16)
            row_dot = jnp.sum(g.astype(F32) * out.astype(F32), axis=1, keepdims=True)
            gw = dot(g, values, ((1,), (1,)))
            ds = (w * (gw - row_dot)).astype(BF16)
            dq = dot(ds, keys, ((1,), (0,))) * inv_root
            out_ref[part] = out.reshape(head_step, BLK, head_size)
            dq_ref[part] = dq.astype(BF16).reshape(head_step, BLK, head_size)
            w_scr[step * step_rows : (step + 1) * step_rows] = w_low
            ds_scr[step * step_rows : (step + 1) * step_rows] = ds
        q_all = q_ref[:, rows(block)].reshape(heads * BLK, head_size)
        g_all = g_ref[:, rows(block)].reshape(heads * BLK, head_size)
        dk = dot(ds_scr[...], q_all, ((0,), (0,))) * inv_root
        dv = dot(w_scr[...], g_all, ((0,), (0,)))
        for position, (_, offset, distance) in enumerate(entries):
            dk_part = dk[position * BLK : (position + 1) * BLK]
            dv_part = dv[position * BLK : (position + 1) * BLK]
            if distance > 0:
                add_pend(distance, block, dk_part, dv_part)
            elif block >= offset:
                add_own(block - offset, dk_part, dv_part)
            else:
                add_pend(1, block - offset + block_count, dk_part, dv_part)

    def forward_grad(distance, block):
        i = place[distance]
        if 2 * distance in place:
            arrives = grad_arrives(2 * distance)

            @pl.when(arrives)
            def _():
                grad_copy(2 * distance, block).wait_recv()
                total = pend_grad[i, rows(block)] + landed[place[2 * distance], rows(block)].astype(F32)
                stage[i, rows(block)] = total.astype(BF16)

            @pl.when(jnp.logical_not(arrives))
            def _():
                stage[i, rows(block)] = pend_grad[i, rows(block)].astype(BF16)
        else:
            stage[i, rows(block)] = pend_grad[i, rows(block)].astype(BF16)

        @pl.when(me >= distance)
        def _():
            grad_copy(distance, block).start()

    def drain(block):
        for distance in reversed(distances[:-1]):
            forward_grad(distance, block)

    def finish(block):
        @pl.when(grad_arrives(1))
        def _():
            grad_copy(1, block).wait_recv()
            own_grad[rows(block)] += landed[place[1], rows(block)].astype(F32)

        dk_ref[0, rows(block)] = own_grad[rows(block), :head_size].astype(BF16)
        dv_ref[0, rows(block)] = own_grad[rows(block), head_size:].astype(BF16)

    last = distances[-1]
    for block in range(block_count):

        @pl.when(me >= last)
        def _(block=block):
            kv_copy(last, block).wait_recv()

        compute(block)
        forward_grad(last, block)
        if block >= 1:
            drain(block - 1)
    drain(block_count - 1)
    for block in range(block_count):
        finish(block)

    for distance in distances:

        @pl.when(kv_sends(distance))
        def _(distance=distance):
            for block in range(block_count):
                kv_copy(distance, block).wait_send()

        @pl.when(me >= distance)
        def _(distance=distance):
            for block in range(block_count):
                grad_copy(distance, block).wait_send()


def local(queries, key_rows, value_rows, out_grad, link_mask):
    heads, row_count, head_size = queries.shape
    block_count = row_count // BLK
    ctx_size = lax.axis_size("ctx")
    entries = slot_table(block_count, ctx_size)
    distances = sorted(set(entry[2] for entry in entries if entry[2] > 0))
    levels = len(distances)
    keys_wide = len(entries) * BLK
    vmem = pl.BlockSpec(memory_space=pltpu.VMEM)
    flops = 10 * heads * row_count * keys_wide * head_size
    return pl.pallas_call(
        functools.partial(kernel, ctx_size, entries, distances),
        out_shape=(
            jax.ShapeDtypeStruct(queries.shape, BF16),
            jax.ShapeDtypeStruct(queries.shape, BF16),
            jax.ShapeDtypeStruct(key_rows.shape, BF16),
            jax.ShapeDtypeStruct(value_rows.shape, BF16),
        ),
        in_specs=[pl.BlockSpec(memory_space=pltpu.SMEM), vmem, vmem, vmem, vmem],
        out_specs=(vmem, vmem, vmem, vmem),
        scratch_shapes=[
            pltpu.VMEM((row_count, 2 * head_size), BF16),
            pltpu.VMEM((levels, row_count, 2 * head_size), BF16),
            pltpu.VMEM((row_count, 2 * head_size), F32),
            pltpu.VMEM((levels, row_count, 2 * head_size), F32),
            pltpu.VMEM((levels, row_count, 2 * head_size), BF16),
            pltpu.VMEM((levels, row_count, 2 * head_size), BF16),
            pltpu.VMEM((heads * BLK, keys_wide), BF16),
            pltpu.VMEM((heads * BLK, keys_wide), BF16),
            pltpu.SemaphoreType.DMA((levels, block_count)),
            pltpu.SemaphoreType.DMA((levels, block_count)),
            pltpu.SemaphoreType.DMA((levels, block_count)),
            pltpu.SemaphoreType.DMA((levels, block_count)),
        ],
        compiler_params=pltpu.CompilerParams(
            collective_id=0, has_side_effects=True, vmem_limit_bytes=56 * 1024 * 1024
        ),
        cost_estimate=pl.CostEstimate(
            flops=flops,
            bytes_accessed=8 * heads * row_count * head_size,
            transcendentals=heads * row_count * keys_wide,
        ),
    )(link_mask, queries, out_grad, key_rows, value_rows)


def solution(mesh):
    return jax.shard_map(
        local,
        mesh=mesh,
        in_specs=(
            P(("groups", "head"), "ctx", None),
            P(("groups", "head"), "ctx", None),
            P(("groups", "head"), "ctx", None),
            P(("groups", "head"), "ctx", None),
            P(("groups", "ctx"), None),
        ),
        out_specs=(
            P(("groups", "head"), "ctx", None),
            P(("groups", "head"), "ctx", None),
            P(("groups", "head"), "ctx", None),
            P(("groups", "head"), "ctx", None),
        ),
        check_vma=False,
    )
```

time: 85.6 us -> 46.3 us (0.54)
  Pallas kernels: 0 us -> 40.4 us
  waiting for transfers between devices: 22.7 us -> 0 us
  matrix products: 14 us -> 0 us
  between operations: 14 us -> 0.65 us
  starting transfers between devices: 12.8 us -> 0 us
  local copies, waits for them, and re-layouts: 13.9 us -> 4.99 us
  other arithmetic: 7.31 us -> 0 us
    pallas_call x0 -> x1, Pallas kernels: none -> 40.4 us  [local(): pl.pallas_call(functools.partial(kernel, ctx_size, entries, distances), o...]
    ppermute x4 -> x0, waiting for transfers between devices: 22.7 us -> none  [from_behind(): lax.ppermute(value, axis, [(source, source + steps) for source in range(f...]
    dot_general x24 -> x0, matrix products: 14 us -> none  [the longest x4 3.01 us: local(): jnp.einsum('hgtd,gkd->hgtk', grad_part, value_part, preferred_element_typ...]
    ppermute x4 -> x0, starting transfers between devices: 12.8 us -> none  [from_behind(): lax.ppermute(value, axis, [(source, source + steps) for source in range(f...]
    unnamed x38 -> x10, local copies, waits for them, and re-layouts: 8.52 us -> 4.99 us
    slice x2 -> x0, local copies, waits for them, and re-layouts: 3.35 us -> none  [local(): link_mask[first_block:last_block, slot_id] == 1]
    concatenate x3 -> x0, other arithmetic: 2.88 us -> none  [the longest x1 1.7 us: local(): key_value = jnp.concatenate([key_rows[0], value_rows[0]], axis=1)]
    reduce_sum x4 -> x0, other arithmetic: 1.44 us -> none  [local(): jnp.sum(jnp.exp(scores - row_max), axis=-1, keepdims=True)]
  transfers between devices with their start and end apart: 4 -> 0, of which waited for: 2 -> 0; matrix products, arithmetic and copies ran while one was open for 16% -> 0% of each run, Pallas kernels for 0% -> 0%
where the time goes in v1:
time: 46.3 us; the launch traced here: 46.1 us
  Pallas kernels  40.4 us (87%)
  local copies, waits for them, and re-layouts  4.99 us (11%)
  between operations  0.65 us (1%)
    pallas_call x1, Pallas kernels, local(): pl.pallas_call(functools.partial(kernel, ctx_size, entries, distances), o...  40.4 us
    unnamed x10, local copies, waits for them, and re-layouts  4.99 us

profile of v1, /device:TPU:0, one launch (start us, length us, event | category | flops | bytes accessed | tf_op | source)
XLA Modules:
  0.0 46.1 jit_solution(6272517099324548113)
XLA Ops:
  0.6 40.4 %shard_map.84 = (bf16[8,512,128]{2,1,0:T(8,128)(2,1)}, bf16[8,512,128]{2,1,0:T(8,128)(2,1)}, bf16[1,512,128]{2,1,0:T(8,128)(2,1)}, bf16[1,512,128]{2,1,0:T(8,128)(2,1)}) custom-call(s32[4,11]{1,0:T(4,128)} %mask_ref.1, bf16[8,512,128]{2,1,0:T(8,128)(2,1)} %q_ref.1, bf16[8,512,128]{2,1,0:T(8,128)(2,1)} %g_ref.1, bf16[1,512,128]{2,1,0:T(8,128)(2,1)} %k_ref.1, ...), custom_call_target="tpu_custom_call" | custom-call | flops 3355443200 | bytes 4194304 | tf_op jit(solution)/shard_map/pallas_call | solution.py:320
  41.1 0.0 copy-start
  41.1 2.4 %copy.13 = bf16[8,512,128]{2,1,0:T(8,128)(2,1)} copy(bf16[8,512,128]{2,1,0:T(8,128)(2,1)} %get-tuple-element.8) | data formatting | bytes 2097152
  43.4 0.0 copy-done
  43.4 0.0 copy-start.2
  43.4 1.0 %copy.14 = bf16[8,512,128]{2,1,0:T(8,128)(2,1)} copy(bf16[8,512,128]{2,1,0:T(8,128)(2,1)S(1)} %copy-done) | data formatting | bytes 2097152
  44.4 0.1 copy-done.2
  44.5 0.0 copy-start.1
  44.5 0.7 %copy.15 = bf16[1,512,128]{2,1,0:T(8,128)(2,1)} copy(bf16[1,512,128]{2,1,0:T(8,128)(2,1)S(1)} %copy-done.2) | data formatting | bytes 262144
  45.1 0.3 copy-done.1
  45.4 0.7 %copy.16 = bf16[1,512,128]{2,1,0:T(8,128)(2,1)} copy(bf16[1,512,128]{2,1,0:T(8,128)(2,1)S(1)} %copy-done.1) | data formatting | bytes 262144
Async XLA Ops:
  41.1 2.4 %copy-start = (bf16[8,512,128]{2,1,0:T(8,128)(2,1)S(1)}, bf16[8,512,128]{2,1,0:T(8,128)(2,1)}, u32[]{:S(2)}) copy-start(bf16[8,512,128]{2,1,0:T(8,128)(2,1)} %get-tuple-element.9) | copy-start | bytes 3145732
  43.4 1.0 %copy-start.2 = (bf16[1,512,128]{2,1,0:T(8,128)(2,1)S(1)}, bf16[1,512,128]{2,1,0:T(8,128)(2,1)}, u32[]{:S(2)}) copy-start(bf16[1,512,128]{2,1,0:T(8,128)(2,1)} %get-tuple-element.10) | copy-start | bytes 393220
  44.5 1.0 %copy-start.1 = (bf16[1,512,128]{2,1,0:T(8,128)(2,1)S(1)}, bf16[1,512,128]{2,1,0:T(8,128)(2,1)}, u32[]{:S(2)}) copy-start(bf16[1,512,128]{2,1,0:T(8,128)(2,1)} %get-tuple-element.11) | copy-start | bytes 393220
